TPU v7x, 512 devices: a whole 4x8x8 slice. The times are simulated.
512 devices in a mesh: row: 64 (over z_hi, y, x), chan: 8 (over z_lo, core).
Axes of the slice: x: 4, y: 8, z: 8 (z_hi: 2, z_lo: 4; z = z_hi * 4 + z_lo), core: 2. Of those that a mesh axis runs over, the one named last changes fastest.
Arguments:
- pair_in: bfloat16 [128, 512, 512], P('chan', 'row'), may hold values from -200 to 200, as said below
- token_mask: int32 [512], replicated, may hold values 0 or 1
- in_gain: bfloat16 [128], P('chan'), may hold values from 0.5 to 1.5
- in_bias: bfloat16 [128], P('chan'), may hold values from -3 to 3
- in_weight: bfloat16 [4, 128, 128], P(None, None, 'chan'), may hold values from -0.5 to 0.5
- out_gain: float32 [128], P('chan'), may hold values from 0.5 to 1.5
- out_bias: float32 [128], P('chan'), may hold values from -3 to 3
- out_weight: bfloat16 [128, 128], replicated, may hold values from -0.5 to 0.5
- gate_weight: bfloat16 [128, 128], P(None, 'chan'), may hold values from -0.5 to 0.5
Outputs:
- result: bfloat16 [128, 512, 512], P('chan', 'row')
Inputs may be any that keep to these rules, and one draw needn't show every extreme that they name: `pair_in`: pair features.
All inputs are finite; a program needn't handle non-finite values.
Results may differ from a plain program's by a relative error of at most 0.0053.
Values may be sent and summed in bfloat16 or wider, within the bound.
A program may use at most 64 MiB of HBM per device.

v0:
```python
import jax
import jax.numpy as jnp
from jax import lax
from jax.sharding import PartitionSpec as P

epsilon = 1e-05


def input_moments(values, total):
    mean = lax.psum(jnp.sum(values, axis=0), "chan") / total
    center = values - mean
    spread = lax.psum(jnp.sum(center * center, axis=0), "chan") / total
    return (center, lax.rsqrt(spread + epsilon))


def output_moments(values, total):
    mean = lax.psum(jnp.sum(values, axis=0), "chan") / total
    center = values - mean
    spread = lax.psum(jnp.sum(center * center, axis=0), "chan") / total
    return (center, lax.rsqrt(spread + epsilon))


def body(
    pair_in, token_mask, in_gain, in_bias, in_weight, out_gain, out_bias, out_weight, gate_weight
):
    rows_local = pair_in.shape[1]
    hidden_local = in_weight.shape[2]
    total_chan = gate_weight.shape[0]
    total_hidden = out_weight.shape[0]
    row_start = lax.axis_index("row") * rows_local
    center, inverse = input_moments(pair_in.astype(jnp.float32), total_chan)
    scaled = (
        center * inverse * in_gain.astype(jnp.float32)[:, None, None]
        + in_bias.astype(jnp.float32)[:, None, None]
    )
    normed = lax.all_gather(scaled.astype(jnp.bfloat16), "chan", axis=0, tiled=True)
    proj = jnp.einsum("pch,crn->phrn", in_weight, normed, preferred_element_type=jnp.float32)
    valid = token_mask.astype(jnp.float32)
    row_valid = lax.dynamic_slice_in_dim(valid, row_start, rows_local)
    pair_mask = row_valid[:, None] * valid[None, :]
    left = (jax.nn.sigmoid(proj[1]) * proj[0] * pair_mask).astype(jnp.bfloat16)
    right = (jax.nn.sigmoid(proj[3]) * proj[2] * pair_mask).astype(jnp.bfloat16)
    triangle = jnp.einsum(
        "cik,cjk->cij",
        left,
        lax.all_gather(right, "row", axis=1, tiled=True),
        preferred_element_type=jnp.float32,
    )
    center_out, inverse_out = output_moments(triangle, total_hidden)
    hidden_norm = (
        center_out * inverse_out * out_gain[:, None, None] + out_bias[:, None, None]
    ).astype(jnp.bfloat16)
    gate = jax.nn.sigmoid(
        jnp.einsum("cd,crn->drn", gate_weight, normed, preferred_element_type=jnp.float32)
    )
    hidden_start = lax.axis_index("chan") * hidden_local
    weight_rows = lax.dynamic_slice_in_dim(out_weight, hidden_start, hidden_local, 0)
    mixed = lax.psum_scatter(
        jnp.einsum("hd,hrn->drn", weight_rows, hidden_norm, preferred_element_type=jnp.float32),
        "chan",
        scatter_dimension=0,
        tiled=True,
    )
    return (mixed * gate).astype(jnp.bfloat16)


def solution(mesh):
    return jax.shard_map(
        body,
        mesh=mesh,
        in_specs=(
            P("chan", "row", None),
            P(),
            P("chan"),
            P("chan"),
            P(None, None, "chan"),
            P("chan"),
            P("chan"),
            P(),
            P(None, "chan"),
        ),
        out_specs=P("chan", "row", None),
        check_vma=False,
    )
```

profile of v0, /device:TPU:1, one launch (start us, length us, event | category | flops | bytes accessed | tf_op | source)
XLA Modules:
  0.0 425.8 jit_solution(13707437953972529163)
XLA Ops:
  6.5 0.7 convert_element_type.28
  7.2 0.7 convert_element_type.29
  7.9 1.0 convert_reduce_fusion
  8.9 28.7 %psum.28 = f32[8,512]{1,0:T(8,128)S(1)} all-reduce(f32[8,512]{1,0:T(8,128)S(1)} %convert_reduce_fusion), channel_id=1, replica_groups=mesh['row'=64,'chan'=8] {'chan'}, use_global_device_ids=true, to_apply=%region_1.0 | all-reduce | flops 4096 | bytes 32768 | tf_op jit(solution)/shard_map/psum | solution.py:10
  37.5 1.0 fusion.11
  38.5 25.9 %psum.29 = f32[8,512]{1,0:T(8,128)S(1)} all-reduce(f32[8,512]{1,0:T(8,128)S(1)} %fusion.11), channel_id=1, replica_groups=mesh['row'=64,'chan'=8] {'chan'}, use_global_device_ids=true, to_apply=%region_3.0 | all-reduce | flops 4096 | bytes 32768 | tf_op jit(solution)/shard_map/psum | solution.py:12
  64.5 1.7 fusion.14
  66.1 0.0 all-gather.5.cloned.1.call-start
  66.2 0.7 convert_element_type.31
  66.9 0.1 dynamic_slice.7
  67.0 0.1 broadcast_multiply_fusion
  67.0 42.5 %all-gather.3.cloned.1.call-done = bf16[128,8,512]{2,0,1:T(8,128)(2,1)} async-done(((bf16[16,8,512]{2,0,1:T(8,128)(2,1)}), bf16[128,8,512]{2,0,1:T(8,128)(2,1)}) %all-gather.3.cloned.1.call-update) | async-done | bytes 1048592 | tf_op jit(solution)/shard_map/all_gather | solution.py:36
  109.5 1.6 convolution_bitcast_fusion
  111.1 0.8 fusion.26
  112.0 0.0 reduce-scatter.2.cloned.1.call-start
  112.0 201.1 %all-gather.5.cloned.1.call-done = bf16[16,512,512]{2,0,1:T(8,128)(2,1)} async-done(((bf16[16,8,512]{2,0,1:T(8,128)(2,1)}), bf16[16,512,512]{2,0,1:T(8,128)(2,1)}) %all-gather.5.cloned.1.call-update) | async-done | bytes 8388624 | tf_op jit(solution)/shard_map/all_gather | solution.py:46
  313.2 12.3 %fusion.39 = (f32[8,512]{1,0:T(8,128)S(1)}, f32[16,8,512]{2,1,0:T(8,128)S(1)}) fusion(bf16[16,512,512]{2,0,1:T(8,128)(2,1)} %all-gather.5.cloned.1.call-done, bf16[16,8,512]{2,0,1:T(8,128)(2,1)S(1)} %get-tuple-element.5), kind=kOutput, calls=%fused_computation.54 | convolution fusion | flops 67170304 | bytes 8798208 | tf_op jit(solution)/shard_map/cik,cjk->cij/dot_general | solution.py:43
  325.5 25.0 %psum.30 = f32[8,512]{1,0:T(8,128)S(1)} all-reduce(f32[8,512]{1,0:T(8,128)S(1)} %get-tuple-element.7), channel_id=1, replica_groups=mesh['row'=64,'chan'=8] {'chan'}, use_global_device_ids=true, to_apply=%region_5.0 | all-reduce | flops 4096 | bytes 32768 | tf_op jit(solution)/shard_map/psum | solution.py:17
  350.5 25.9 %psum.31 = f32[8,512]{1,0:T(8,128)S(1)} all-reduce(f32[8,512]{1,0:T(8,128)S(1)} %multiply_reduce_fusion), channel_id=1, replica_groups=mesh['row'=64,'chan'=8] {'chan'}, use_global_device_ids=true, to_apply=%region_7.0 | all-reduce | flops 4096 | bytes 32768 | tf_op jit(solution)/shard_map/psum | solution.py:19
  376.4 0.1 add_convert_fusion
  376.5 1.8 fusion.31
  378.4 38.9 %reduce-scatter.2.cloned.1.call-done = f32[16,8,512]{2,0,1:T(8,128)} async-done(((f32[128,8,512]{2,0,1:T(8,128)}), f32[16,8,512]{2,0,1:T(8,128)}) %reduce-scatter.2.cloned.1.call-update) | async-done | bytes 262160 | tf_op jit(solution)/shard_map/reduce_scatter | solution.py:58
  417.3 1.2 fusion.7
  418.5 0.7 copy.27
  (19 shorter events, 0.1 us)
Async XLA Ops:
  6.5 370.0 %copy-start = (bf16[128,128]{1,0:T(8,128)(2,1)S(1)}, bf16[128,128]{1,0:T(8,128)(2,1)}, u32[]{:S(2)}) copy-start(bf16[128,128]{1,0:T(8,128)(2,1)} %param.16) | copy-start | bytes 98308
  6.5 369.9 %copy-start.2 = (f32[16]{0:T(128)S(1)}, f32[16]{0:T(128)}, u32[]{:S(2)}) copy-start(f32[16]{0:T(128)} %param.15) | copy-start | bytes 196
  6.5 369.9 %copy-start.3 = (f32[16]{0:T(128)S(1)}, f32[16]{0:T(128)}, u32[]{:S(2)}) copy-start(f32[16]{0:T(128)} %param.14) | copy-start | bytes 196
  6.5 103.0 %all-gather.3.cloned.1.call-start = ((), (), s32[]{:S(2)}) async-start(), calls=%async_computation.1 | async-start | bytes 1179648 | tf_op jit(solution)/shard_map/all_gather | solution.py:36
  66.1 247.0 %all-gather.5.cloned.1.call-start = ((), (), s32[]{:S(2)}) async-start(), calls=%async_computation.2 | async-start | bytes 8519680 | tf_op jit(solution)/shard_map/all_gather | solution.py:46
  67.0 350.3 %copy-start.4 = (bf16[128,16]{0,1:T(8,128)(2,1)S(1)}, bf16[128,16]{0,1:T(8,128)(2,1)}, u32[]{:S(2)}) copy-start(bf16[128,16]{0,1:T(8,128)(2,1)} %param.17) | copy-start | bytes 12292
  109.5 307.8 %copy-start.1 = (bf16[128,8,512]{2,0,1:T(8,128)(2,1)S(1)}, bf16[128,8,512]{2,0,1:T(8,128)(2,1)}, u32[]{:S(2)}) copy-start(bf16[128,8,512]{2,0,1:T(8,128)(2,1)} %all-gather.3.cloned.1.call-done) | copy-start | bytes 3145732
  112.0 305.3 %reduce-scatter.2.cloned.1.call-start = ((), (), s32[]{:S(2)}) async-start(), calls=%async_computation.3 | async-start | bytes 2359296 | tf_op jit(solution)/shard_map/reduce_scatter | solution.py:58
Sparse Core Ops, SparseCore 0:
  66.3 43.1 all-gather.2
  114.0 199.1 all-gather.4
  378.5 38.7 reduce-scatter.1
where the time goes:
time: 428 us; the launch traced here: 426 us
  waiting for transfers between devices  283 us (66%)
  blocking collectives  105 us (25%)
  matrix products  17 us (4%)
  between operations  13.2 us (3%)
  other arithmetic  6.68 us (2%)
    all_gather x1, waiting for transfers between devices, body(): lax.all_gather(right, 'row', axis=1, tiled=True)  201 us
    all_gather x1, waiting for transfers between devices, body(): lax.all_gather(scaled.astype(jnp.bfloat16), 'chan', axis=0, tiled=True)  42.5 us
    reduce_scatter x1, waiting for transfers between devices, body(): lax.psum_scatter(jnp.einsum('hd,hrn->drn', weight_rows, hidden_norm, pref...  38.9 us
    psum x1, blocking collectives, input_moments(): mean = lax.psum(jnp.sum(values, axis=0), 'chan') / total  28.7 us
    psum x1, blocking collectives, input_moments(): spread = lax.psum(jnp.sum(center * center, axis=0), 'chan') / total  25.9 us
    psum x1, blocking collectives, output_moments(): spread = lax.psum(jnp.sum(center * center, axis=0), 'chan') / total  25.9 us
    psum x1, blocking collectives, output_moments(): mean = lax.psum(jnp.sum(values, axis=0), 'chan') / total  25 us
    dot_general x1, matrix products, body(): jnp.einsum('cik,cjk->cij', left, lax.all_gather(right, 'row', axis=1, til...  12.3 us
  transfers between devices with their start and end apart: 3, of which 3 were waited for; matrix products, arithmetic and copies ran while one was open for 0% of the time, Pallas kernels for 0%

commit v1 on v0

v1 whole, which is shorter than its diff:
```python
import jax
import jax.numpy as jnp
from jax import lax
from jax.experimental import pallas as pl
from jax.experimental.pallas import tpu as pltpu
from jax.sharding import PartitionSpec as P

MESH = pl.DeviceIdType.MESH
EPS = 1e-05
NZH, NY, NX, NZL, NC = 2, 8, 4, 4, 2
NCH = NZL * NC
T = 4
KC = 128
F32 = jnp.float32
BF16 = jnp.bfloat16


def dot(a, b):
    return jnp.dot(a, b, preferred_element_type=F32)


def column(vec):
    n = vec.shape[1]
    a = lax.broadcasted_iota(jnp.int32, (n, n), 0)
    b = lax.broadcasted_iota(jnp.int32, (n, n), 1)
    return jnp.sum(jnp.where(a == b, jnp.broadcast_to(vec, (n, n)), 0.0), axis=1, keepdims=True)


def kernel(
    pair, tm_s, tm_v, ig, ib, w, og, ob, wo, gw,
    out,
    xf, xb, pm, gb, lr_f, lb, rb, acc, e_f, es, er, fs, fr, gate, perm, wot, o_f,
    xs_sem, xr_sem, ps_sem, pr_sem, ls_sem, lr_sem, rs_sem, rr_sem, es_sem, er_sem, fs_sem, fr_sem,
):
    row = lax.axis_index("row")
    chan = lax.axis_index("chan")
    zh = lax.div(row, NY * NX)
    y = lax.rem(lax.div(row, NX), NY)
    x = lax.rem(row, NX)
    zl = lax.div(chan, NC)
    core = lax.rem(chan, NC)
    me_m = zh * NX + x

    def row_of(zh_, y_, x_):
        return (zh_ * NY + y_) * NX + x_

    def yrow(d):
        return row_of(zh, lax.rem(y + (NY + d), NY), x)

    def xrow(d):
        return row_of(zh, y, lax.rem(x + (NX + d), NX))

    row_z = row_of(1 - zh, y, x)
    row_f = row_of(lax.div(chan, NX), y, lax.rem(chan, NX))
    self_f = me_m == chan
    sibling = zl * NC + (1 - core)

    bar = pltpu.get_barrier_semaphore()

    def greet(r, c):
        pl.semaphore_signal(bar, inc=1, device_id=(r, c), device_id_type=MESH)

    for s in range(1, NCH):
        greet(row, lax.rem(chan + s, NCH))
    for r in (yrow(1), yrow(-1), xrow(1), xrow(-1), row_z):
        greet(r, chan)
    for s in range(1, NCH):
        m = lax.rem(me_m + s, NCH)
        greet(row_of(lax.div(m, NX), y, lax.rem(m, NX)), me_m)

    @pl.when(jnp.logical_not(self_f))
    def _():
        greet(row, me_m)

    sends = []

    def send(src, dst, ssem, rsem, r, c):
        copy = pltpu.make_async_remote_copy(
            src_ref=src, dst_ref=dst, send_sem=ssem, recv_sem=rsem,
            device_id=(r, c), device_id_type=MESH,
        )
        copy.start()
        sends.append(copy)

    def arrived(ref, ssem, rsem):
        pltpu.make_async_remote_copy(
            src_ref=ref, dst_ref=ref, send_sem=ssem, recv_sem=rsem,
            device_id=(row, sibling), device_id_type=MESH,
        ).wait_recv()

    for t in range(T):
        xf[t] = pair[:, :, t * KC:(t + 1) * KC].astype(F32).reshape(128, KC)
        for r in range(8):
            xb[t, chan, r] = xf[t, pl.ds(r, 16, stride=8), :].astype(BF16)
    lane16 = lax.broadcasted_iota(jnp.int32, (16, 128), 1)
    cols = [column(v[...].astype(F32)) for v in (ig, ib, og, ob)]
    block = jnp.zeros((16, 128), F32)
    for n, col in enumerate(cols):
        block = jnp.where(lane16 == n, jnp.broadcast_to(col, (16, 128)), block)
    pm[chan] = block

    pl.semaphore_wait(bar, jnp.where(self_f, 2 * NCH + 3, 2 * NCH + 4))

    for s in range(1, NCH):
        send(pm.at[chan], pm.at[chan], ps_sem.at[s], pr_sem.at[chan], row, lax.rem(chan + s, NCH))
    for t in range(T):
        for d in range(1, NZL):
            c = lax.rem(zl + d, NZL) * NC + core
            send(xb.at[t, chan], xb.at[t, chan], xs_sem.at[t, d], xr_sem.at[t, chan], row, c)
        send(xb.at[t, chan], xb.at[t, chan], xs_sem.at[t, 0], xr_sem.at[t, chan], row, sibling)

    ki = lax.broadcasted_iota(jnp.int32, (512, 512), 0)
    ni = lax.broadcasted_iota(jnp.int32, (512, 512), 1)
    kx, ky, kp, k8 = ki >> 7, (ki >> 4) & 7, (ki >> 3) & 1, ki & 7
    want = (kp << 8) | (ky << 5) | (kx << 3) | k8
    perm[...] = jnp.where(want == ni, 1.0, 0.0).astype(BF16)
    eye_a = lax.broadcasted_iota(jnp.int32, (128, 128), 0)
    eye_b = lax.broadcasted_iota(jnp.int32, (128, 128), 1)
    eye = jnp.where(eye_a == eye_b, 1.0, 0.0).astype(BF16)
    turned = lax.dot_general(eye, wo[...], (((1,), (1,)), ((), ())), preferred_element_type=F32).astype(BF16)
    ha = lax.broadcasted_iota(jnp.int32, (128, 64), 0)
    hb = lax.broadcasted_iota(jnp.int32, (128, 64), 1)
    for par in range(2):
        pick = jnp.where(ha == 2 * hb + par, 1.0, 0.0).astype(BF16)
        wot[par * 128:(par + 1) * 128, :] = dot(turned, pick).astype(BF16)

    wt = jnp.concatenate([w[...].reshape(64, 128), gw[...]], axis=0)
    for s in range(1, NCH):
        c = lax.rem(chan + s, NCH)
        arrived(pm.at[c], ps_sem.at[s], pr_sem.at[c])
    pmv = pm[...].reshape(128, 128)
    gb[0] = jnp.broadcast_to(pmv[:, 0:1], (128, 128))
    gb[1] = jnp.broadcast_to(pmv[:, 1:2], (128, 128))
    row_valid = [tm_s[row * 8 + r].astype(F32) for r in range(8)]

    def gather_in(t):
        for d in range(1, NZL):
            c = lax.rem(zl + d, NZL) * NC + core
            arrived(xb.at[t, c], xs_sem.at[t, 0], xr_sem.at[t, c])
            send(xb.at[t, c], xb.at[t, c], xs_sem.at[t, 3 + d], xr_sem.at[t, c], row, sibling)
        for d in range(NZL):
            c = lax.rem(zl + d, NZL) * NC + (1 - core)
            arrived(xb.at[t, c], xs_sem.at[t, 0], xr_sem.at[t, c])

    def project(t):
        pieces = []
        gain = gb[0]
        bias = gb[1]
        for r in range(8):
            v = xb[t, :, r].astype(F32).reshape(128, KC)
            mean = jnp.sum(v, axis=0, keepdims=True) * (1.0 / 128)
            center = v - mean
            spread = jnp.sum(center * center, axis=0, keepdims=True) * (1.0 / 128)
            pieces.append((center * lax.rsqrt(spread + EPS) * gain + bias).astype(BF16))
        normed = jnp.concatenate(pieces, axis=1)
        proj = dot(wt, normed)
        col_valid = tm_v[:, t * KC:(t + 1) * KC].astype(F32)
        mask = jnp.concatenate([col_valid * s for s in row_valid], axis=1)
        left = jax.nn.sigmoid(proj[16:32]) * proj[0:16] * mask
        right = jax.nn.sigmoid(proj[48:64]) * proj[32:48] * mask
        g = jax.nn.sigmoid(proj[64:80])
        for r in range(8):
            lr_f[0, pl.ds(r, 16, stride=8), :] = left[:, r * KC:(r + 1) * KC]
            lr_f[1, pl.ds(r, 16, stride=8), :] = right[:, r * KC:(r + 1) * KC]
            gate[r, :, t * KC:(t + 1) * KC] = g[:, r * KC:(r + 1) * KC]
        lb[t, me_m] = lr_f[0].astype(BF16)
        rb[t, y] = lr_f[1].astype(BF16)

    def lslot(far, d):
        return (1 - zh if far else zh) * NX + lax.rem(x + (NX + d), NX)

    def rslot(d):
        return lax.rem(y + (NY + d), NY)

    def send_l(t, n, slot, r):
        send(lb.at[t, slot], lb.at[t, slot], ls_sem.at[t, n], lr_sem.at[t, slot], r, chan)

    def send_r(t, n, slot, r):
        send(rb.at[t, slot], rb.at[t, slot], rs_sem.at[t, n], rr_sem.at[t, slot], r, chan)

    def got_l(t, slot):
        arrived(lb.at[t, slot], ls_sem.at[t, 0], lr_sem.at[t, slot])

    def got_r(t, slot):
        arrived(rb.at[t, slot], rs_sem.at[t, 0], rr_sem.at[t, slot])

    def step1(t):
        send_l(t, 0, me_m, row_z)
        send_r(t, 0, y, yrow(1))
        send_r(t, 1, y, yrow(-1))
        send_l(t, 1, me_m, xrow(1))
        send_l(t, 2, me_m, xrow(-1))

    def step2(t):
        got_r(t, rslot(-1))
        send_r(t, 2, rslot(-1), yrow(1))
        got_r(t, rslot(1))
        send_r(t, 3, rslot(1), yrow(-1))
        got_l(t, lslot(False, -1))
        got_l(t, lslot(False, 1))
        if t % 2 == 0:
            send_l(t, 3, lslot(False, -1), xrow(1))
        else:
            send_l(t, 3, lslot(False, 1), xrow(-1))
        got_l(t, lslot(True, 0))
        send_l(t, 4, lslot(True, 0), xrow(1))
        send_l(t, 5, lslot(True, 0), xrow(-1))

    def step3(t):
        got_r(t, rslot(-2))
        send_r(t, 4, rslot(-2), yrow(1))
        got_r(t, rslot(2))
        send_r(t, 5, rslot(2), yrow(-1))
        got_l(t, lslot(True, -1))
        got_l(t, lslot(True, 1))
        if t % 2 == 0:
            send_l(t, 6, lslot(True, 1), xrow(-1))
        else:
            send_l(t, 6, lslot(True, -1), xrow(1))

    def step4(t):
        got_r(t, rslot(-3))
        got_r(t, rslot(3))
        if t % 2 == 0:
            send_r(t, 6, rslot(-3), yrow(1))
        else:
            send_r(t, 6, rslot(3), yrow(-1))

    def step5(t):
        got_l(t, lslot(False, 2))
        got_l(t, lslot(True, 2))
        got_r(t, rslot(4))
        for h in range(8):
            a = lb[t, :, 16 * h:16 * h + 16, :].reshape(128, KC)
            b = rb[t, :, 16 * h:16 * h + 16, :].reshape(128, KC)
            part = lax.dot_general(a, b, (((1,), (1,)), ((), ())), preferred_element_type=F32)
            if t == 0:
                acc[h] = part
            else:
                acc[h] += part

    for wave in range(T + 4):
        if wave < T:
            gather_in(wave)
            project(wave)
            step1(wave)
        for back, step in ((4, step5), (3, step4), (2, step3), (1, step2)):
            if 0 <= wave - back < T:
                step(wave - back)

    lane = lax.broadcasted_iota(jnp.int32, (1, 128), 1)
    even = ((lane >> 3) & 1) == 0

    for h in range(8):
        o = acc[h].reshape(8, 2, 8, 128)
        own = jnp.where(even, o[:, 0].reshape(64, 128), o[:, 1].reshape(64, 128))
        e_f[pl.ds(h, 64, stride=8), :] = own
    es[...] = e_f[...].astype(BF16).reshape(8, 64, 128)
    for s in range(1, NCH):
        c = lax.rem(chan + s, NCH)
        send(es.at[c], er.at[chan], es_sem.at[s], er_sem.at[chan], row, c)
    er[chan] = es[chan]
    for s in range(1, NCH):
        c = lax.rem(chan + s, NCH)
        arrived(er.at[c], es_sem.at[s], er_sem.at[c])

    tri = er[...].astype(F32).reshape(8, 8, 8, 128)

    def across(v):
        return v + jnp.where(even, pltpu.roll(v, 120, 1), pltpu.roll(v, 8, 1))

    mean = across(jnp.sum(jnp.sum(tri, axis=0), axis=1)) * (1.0 / 128)
    center = tri - mean[None, :, None, :]
    spread = across(jnp.sum(jnp.sum(center * center, axis=0), axis=1)) * (1.0 / 128)
    inverse = lax.rsqrt(spread + EPS)
    e_f[0:128, :] = pmv
    g_e = e_f[pl.ds(0, 64, stride=2), :]
    g_o = e_f[pl.ds(1, 64, stride=2), :]
    gain = jnp.where(even, g_e[:, 2:3], g_o[:, 2:3])
    bias = jnp.where(even, g_e[:, 3:4], g_o[:, 3:4])
    hidden = jnp.concatenate(
        [
            (center[:, r].reshape(64, 128) * inverse[r:r + 1] * gain + bias).astype(BF16)
            for r in range(8)
        ],
        axis=1,
    )
    both = dot(wot[...], hidden)
    for q in range(4):
        a0 = both[0:128, 256 * q:256 * q + 128]
        a1 = both[0:128, 256 * q + 128:256 * q + 256]
        b0 = both[128:256, 256 * q:256 * q + 128]
        b1 = both[128:256, 256 * q + 128:256 * q + 256]
        mixed = jnp.where(even, a0 + pltpu.roll(b0, 120, 1), b1 + pltpu.roll(a1, 8, 1))
        fs[:, q] = mixed.astype(BF16).reshape(8, 16, 128)

    def f_copy():
        return pltpu.make_async_remote_copy(
            src_ref=fs.at[chan], dst_ref=fr.at[me_m], send_sem=fs_sem.at[0], recv_sem=fr_sem.at[me_m],
            device_id=(row_f, chan), device_id_type=MESH,
        )

    for s in range(1, NCH):
        c = lax.rem(chan + s, NCH)
        send(fs.at[c], fr.at[me_m], fs_sem.at[s], fr_sem.at[me_m], row_f, c)

    @pl.when(jnp.logical_not(self_f))
    def _():
        f_copy().start()

    @pl.when(self_f)
    def _():
        fr[me_m] = fs[chan]

    for s in range(1, NCH):
        m = lax.rem(me_m + s, NCH)
        arrived(fr.at[m], fs_sem.at[s], fr_sem.at[m])

    @pl.when(jnp.logical_not(self_f))
    def _():
        arrived(fr.at[me_m], fs_sem.at[0], fr_sem.at[me_m])

    for z in range(NZH):
        got = jnp.concatenate([fr[z * NX + i].reshape(64, 128) for i in range(NX)], axis=1)
        o = dot(got, perm[...])
        for q in range(4):
            for par in range(2):
                r = 2 * q + par
                val = o[16 * q:16 * q + 16, 256 * par:256 * par + 256] * gate[r, :, 256 * z:256 * z + 256]
                for half in range(2):
                    o_f[2 * z + half, pl.ds(r, 16, stride=8), :] = val[:, 128 * half:128 * half + 128]
    for n in range(4):
        out[:, :, 128 * n:128 * n + 128] = o_f[n].reshape(16, 8, 128).astype(BF16)

    for copy in sends:
        copy.wait_send()

    @pl.when(jnp.logical_not(self_f))
    def _():
        f_copy().wait_send()


def body(pair_in, token_mask, in_gain, in_bias, in_weight, out_gain, out_bias, out_weight, gate_weight):
    vm = pl.BlockSpec(memory_space=pltpu.VMEM)
    sm = pl.BlockSpec(memory_space=pltpu.SMEM)
    dma = pltpu.SemaphoreType.DMA
    return pl.pallas_call(
        kernel,
        out_shape=jax.ShapeDtypeStruct((16, 8, 512), BF16),
        in_specs=[vm, sm] + [vm] * 8,
        out_specs=vm,
        scratch_shapes=[
            pltpu.VMEM((T, 128, KC), F32),
            pltpu.VMEM((T, NCH, 8, 16, KC), BF16),
            pltpu.VMEM((NCH, 16, 128), F32),
            pltpu.VMEM((2, 128, 128), F32),
            pltpu.VMEM((2, 128, KC), F32),
            pltpu.VMEM((T, 8, 128, KC), BF16),
            pltpu.VMEM((T, 8, 128, KC), BF16),
            pltpu.VMEM((8, 128, 128), F32),
            pltpu.VMEM((512, 128), F32),
            pltpu.VMEM((8, 64, 128), BF16),
            pltpu.VMEM((8, 64, 128), BF16),
            pltpu.VMEM((8, 4, 16, 128), BF16),
            pltpu.VMEM((8, 4, 16, 128), BF16),
            pltpu.VMEM((8, 16, 512), F32),
            pltpu.VMEM((512, 512), BF16),
            pltpu.VMEM((256, 64), BF16),
            pltpu.VMEM((4, 128, 128), F32),
            dma((T, 7)), dma((T, NCH)),
            dma((NCH,)), dma((NCH,)),
            dma((T, 7)), dma((T, 8)),
            dma((T, 7)), dma((T, 8)),
            dma((NCH,)), dma((NCH,)),
            dma((NCH,)), dma((NCH,)),
        ],
        compiler_params=pltpu.CompilerParams(
            collective_id=0, has_side_effects=True, vmem_limit_bytes=48 * 1024 * 1024
        ),
    )(
        pair_in,
        token_mask,
        token_mask.reshape(1, 512),
        in_gain.reshape(1, 16),
        in_bias.reshape(1, 16),
        jnp.transpose(in_weight, (0, 2, 1)),
        out_gain.reshape(1, 16),
        out_bias.reshape(1, 16),
        out_weight,
        gate_weight.T,
    )


def solution(mesh):
    return jax.shard_map(
        body,
        mesh=mesh,
        in_specs=(
            P("chan", "row", None),
            P(),
            P("chan"),
            P("chan"),
            P(None, None, "chan"),
            P("chan"),
            P("chan"),
            P(),
            P(None, "chan"),
        ),
        out_specs=P("chan", "row", None),
        check_vma=False,
    )
```

time: 428 us -> 70.4 us (0.16)
  waiting for transfers between devices: 283 us -> 0 us
  blocking collectives: 105 us -> 0 us
  Pallas kernels: 0 us -> 66.4 us
  matrix products: 17 us -> 0 us
  between operations: 13.2 us -> 0.04 us
  other arithmetic: 6.68 us -> 0 us
    all_gather x2 -> x0, waiting for transfers between devices: 244 us -> none  [the longest x1 201 us: body(): lax.all_gather(right, 'row', axis=1, tiled=True)]
    psum x4 -> x0, blocking collectives: 105 us -> none  [the longest x1 28.7 us: input_moments(): mean = lax.psum(jnp.sum(values, axis=0), 'chan') / total]
    pallas_call x0 -> x1, Pallas kernels: none -> 66.4 us  [body(): pl.pallas_call(kernel, out_shape=jax.ShapeDtypeStruct((16, 8, 512), BF16)...]
    reduce_scatter x1 -> x0, waiting for transfers between devices: 38.9 us -> none  [body(): lax.psum_scatter(jnp.einsum('hd,hrn->drn', weight_rows, hidden_norm, pref...]
    dot_general x4 -> x0, matrix products: 17 us -> none  [the longest x1 12.3 us: body(): jnp.einsum('cik,cjk->cij', left, lax.all_gather(right, 'row', axis=1, til...]
    convert_element_type x6 -> x0, other arithmetic: 4.59 us -> none  [the longest x1 1.65 us: body(): scaled.astype(jnp.bfloat16)]
  transfers between devices with their start and end apart: 3 -> 0, of which waited for: 3 -> 0; matrix products, arithmetic and copies ran while one was open for 0% -> 0% of each run, Pallas kernels for 0% -> 0%
where the time goes in v1:
time: 70.4 us; the launch traced here: 70.2 us
  Pallas kernels  66.4 us (94%)
  local copies, waits for them, and re-layouts  3.74 us (5%)
    pallas_call x1, Pallas kernels, body(): pl.pallas_call(kernel, out_shape=jax.ShapeDtypeStruct((16, 8, 512), BF16)...  66.4 us
    unnamed x19, local copies, waits for them, and re-layouts  3.74 us

profile of v1, /device:TPU:1, one launch (start us, length us, event | category | flops | bytes accessed | tf_op | source)
XLA Modules:
  0.0 70.2 jit_solution(13355739560205402033)
XLA Ops:
  0.0 0.0 copy-start.8
  0.0 0.0 copy-start.4
  0.0 0.0 copy-start.3
  0.0 0.0 copy-start.5
  0.0 0.0 copy-start.6
  0.0 0.0 copy-start.7
  0.0 0.6 copy-done.8
  0.7 0.0 copy-done.4
  0.7 0.0 copy-done.3
  0.7 0.0 copy-done.5
  0.7 0.0 copy-done.6
  0.7 0.0 copy-done.7
  0.7 0.0 copy-start
  0.7 0.9 %copy-done = bf16[16,8,512]{2,1,0:T(8,128)(2,1)S(1)} copy-done((bf16[16,8,512]{2,1,0:T(8,128)(2,1)S(1)}, bf16[16,8,512]{2,1,0:T(8,128)(2,1)}, u32[]{:S(2)}) %copy-start) | copy-done | bytes 131096
  1.6 0.0 copy-start.1
  1.6 0.8 %copy-done.1 = bf16[128,128]{1,0:T(8,128)(2,1)S(1)} copy-done((bf16[128,128]{1,0:T(8,128)(2,1)S(1)}, bf16[128,128]{1,0:T(8,128)(2,1)}, u32[]{:S(2)}) %copy-start.1) | copy-done | bytes 32792
  2.4 0.0 copy-start.2
  2.4 0.7 %copy-done.2 = bf16[4,128,16]{1,2,0:T(8,128)(2,1)S(1)} copy-done((bf16[4,128,16]{1,2,0:T(8,128)(2,1)S(1)}, bf16[4,128,16]{1,2,0:T(8,128)(2,1)}, u32[]{:S(2)}) %copy-start.2) | copy-done | bytes 16408
  3.1 66.4 %shard_map.91 = bf16[16,8,512]{2,1,0:T(8,128)(2,1)S(1)} custom-call(bf16[16,8,512]{2,1,0:T(8,128)(2,1)S(1)} %copy-done, s32[512]{0:T(512)S(1)} %copy-done.3, s32[1,512]{1,0:T(1,128)S(1)} %bitcast.8, bf16[1,16]{1,0:T(2,128)(2,1)S(1)} %bitcast.10, bf16[1,16]{1,0:T(2,128)(2,1)S(1)} %bitcast.11, bf16[4,16,128]{2,1,0:T(8,128)(2,1)S(1)} %bitcast.7, ...), custom_call_target="tpu_custom_call" | custom-call | tf_op jit(solution)/shard_map/pallas_call | solution.py:347
  69.5 0.7 copy.11
Async XLA Ops:
  0.0 0.7 copy-start.8
  0.0 0.7 copy-start.4
  0.0 0.7 %copy-start.3 = (s32[512]{0:T(512)S(1)}, s32[512]{0:T(512)}, u32[]{:S(2)}) copy-start(s32[512]{0:T(512)} %tm_s.1) | copy-start | bytes 6148
  0.0 0.7 %copy-start.5 = (bf16[16]{0:T(256)(128)(2,1)S(1)}, bf16[16]{0:T(256)(128)(2,1)}, u32[]{:S(2)}) copy-start(bf16[16]{0:T(256)(128)(2,1)} %param.11) | copy-start | bytes 100
  0.0 0.7 copy-start.6
  0.0 0.7 %copy-start.7 = (f32[16]{0:T(128)S(1)}, f32[16]{0:T(128)}, u32[]{:S(2)}) copy-start(f32[16]{0:T(128)} %param.14) | copy-start | bytes 196
  0.7 0.9 %copy-start = (bf16[16,8,512]{2,1,0:T(8,128)(2,1)S(1)}, bf16[16,8,512]{2,1,0:T(8,128)(2,1)}, u32[]{:S(2)}) copy-start(bf16[16,8,512]{2,1,0:T(8,128)(2,1)} %pair.1) | copy-start | bytes 393220
  1.6 0.8 %copy-start.1 = (bf16[128,128]{1,0:T(8,128)(2,1)S(1)}, bf16[128,128]{1,0:T(8,128)(2,1)}, u32[]{:S(2)}) copy-start(bf16[128,128]{1,0:T(8,128)(2,1)} %wo.1) | copy-start | bytes 98308
  2.4 0.7 %copy-start.2 = (bf16[4,128,16]{1,2,0:T(8,128)(2,1)S(1)}, bf16[4,128,16]{1,2,0:T(8,128)(2,1)}, u32[]{:S(2)}) copy-start(bf16[4,128,16]{1,2,0:T(8,128)(2,1)} %param.13) | copy-start | bytes 49156

commit v2 on v1

--- a/solution.py
+++ b/solution.py
@@ -11,6 +11,7 @@
 NCH = NZL * NC
 T = 4
 KC = 128
+AHEAD = 2
 F32 = jnp.float32
 BF16 = jnp.bfloat16
 
@@ -27,11 +28,21 @@
 
 
 def kernel(
-    pair, tm_s, tm_v, ig, ib, w, og, ob, wo, gw,
-    out,
+    tm_s, *refs,
+):
+    ins, (out, *vins), (sem_in, *rest) = refs[:9], refs[9:19], refs[19:]
+    run(tm_s, ins, out, vins, sem_in, *rest)
+
+
+def run(
+    tm_s, ins, out, vins, sem_in,
     xf, xb, pm, gb, lr_f, lb, rb, acc, e_f, es, er, fs, fr, gate, perm, wot, o_f,
     xs_sem, xr_sem, ps_sem, pr_sem, ls_sem, lr_sem, rs_sem, rr_sem, es_sem, er_sem, fs_sem, fr_sem,
 ):
+    loads = [pltpu.make_async_copy(a, b, sem_in.at[n]) for n, (a, b) in enumerate(zip(ins, vins))]
+    for load in loads:
+        load.start()
+    pair, tm_v, ig, ib, w, og, ob, wo, gw = vins
     row = lax.axis_index("row")
     chan = lax.axis_index("chan")
     zh = lax.div(row, NY * NX)
@@ -54,6 +65,10 @@
     row_f = row_of(lax.div(chan, NX), y, lax.rem(chan, NX))
     self_f = me_m == chan
     sibling = zl * NC + (1 - core)
+    z_two = lax.rem(zl + 2, NZL)
+    z_pair = zl + 1 - 2 * lax.rem(zl, 2)
+    z_inner = NZL - 1 - zl
+    inner = jnp.logical_and(zl > 0, zl < NZL - 1)
 
     bar = pltpu.get_barrier_semaphore()
 
@@ -62,31 +77,40 @@
 
     for s in range(1, NCH):
         greet(row, lax.rem(chan + s, NCH))
-    for r in (yrow(1), yrow(-1), xrow(1), xrow(-1), row_z):
+    for r in (yrow(2), yrow(-2), xrow(2), yrow(1), yrow(-1), xrow(1), xrow(-1)):
         greet(r, chan)
-    for s in range(1, NCH):
-        m = lax.rem(me_m + s, NCH)
-        greet(row_of(lax.div(m, NX), y, lax.rem(m, NX)), me_m)
-
-    @pl.when(jnp.logical_not(self_f))
-    def _():
-        greet(row, me_m)
+    at_z = 4 * zh + zl + jnp.where(zl < 2, 7 - zl, 12 - zl)
+    greet(row_of(lax.rem(lax.div(at_z, NZL), NZH), y, x), lax.rem(at_z, NZL) * NC + core)
 
     sends = []
 
-    def send(src, dst, ssem, rsem, r, c):
+    def send(src, dst, ssem, rsem, r, c, when=None):
         copy = pltpu.make_async_remote_copy(
             src_ref=src, dst_ref=dst, send_sem=ssem, recv_sem=rsem,
             device_id=(r, c), device_id_type=MESH,
         )
-        copy.start()
-        sends.append(copy)
+        if when is None:
+            copy.start()
+        else:
+            pl.when(when)(copy.start)
+        sends.append((copy, when))
+
+    def drain(keep):
+        while len(sends) > keep:
+            copy, when = sends.pop(0)
+            if when is None:
+                copy.wait_send()
+            else:
+                pl.when(when)(copy.wait_send)
 
     def arrived(ref, ssem, rsem):
         pltpu.make_async_remote_copy(
             src_ref=ref, dst_ref=ref, send_sem=ssem, recv_sem=rsem,
             device_id=(row, sibling), device_id_type=MESH,
         ).wait_recv()
+
+    for load in loads:
+        load.wait()
 
     for t in range(T):
         xf[t] = pair[:, :, t * KC:(t + 1) * KC].astype(F32).reshape(128, KC)
@@ -99,15 +123,18 @@
         block = jnp.where(lane16 == n, jnp.broadcast_to(col, (16, 128)), block)
     pm[chan] = block
 
-    pl.semaphore_wait(bar, jnp.where(self_f, 2 * NCH + 3, 2 * NCH + 4))
+    pl.semaphore_wait(bar, jnp.where(inner, NCH - 1 + 7, NCH - 1 + 7 + 2))
 
     for s in range(1, NCH):
         send(pm.at[chan], pm.at[chan], ps_sem.at[s], pr_sem.at[chan], row, lax.rem(chan + s, NCH))
-    for t in range(T):
-        for d in range(1, NZL):
-            c = lax.rem(zl + d, NZL) * NC + core
-            send(xb.at[t, chan], xb.at[t, chan], xs_sem.at[t, d], xr_sem.at[t, chan], row, c)
+
+    def send_in(t):
+        for n, (z, when) in enumerate(((z_two, None), (z_inner, inner), (z_pair, None))):
+            send(xb.at[t, chan], xb.at[t, chan], xs_sem.at[t, 1 + n], xr_sem.at[t, chan], row, z * NC + core, when)
         send(xb.at[t, chan], xb.at[t, chan], xs_sem.at[t, 0], xr_sem.at[t, chan], row, sibling)
+
+    for t in range(AHEAD):
+        send_in(t)
 
     ki = lax.broadcasted_iota(jnp.int32, (512, 512), 0)
     ni = lax.broadcasted_iota(jnp.int32, (512, 512), 1)
@@ -134,10 +161,12 @@
     row_valid = [tm_s[row * 8 + r].astype(F32) for r in range(8)]
 
     def gather_in(t):
-        for d in range(1, NZL):
-            c = lax.rem(zl + d, NZL) * NC + core
+        for n, z in enumerate((z_two, z_pair, z_inner)):
+            c = z * NC + core
             arrived(xb.at[t, c], xs_sem.at[t, 0], xr_sem.at[t, c])
-            send(xb.at[t, c], xb.at[t, c], xs_sem.at[t, 3 + d], xr_sem.at[t, c], row, sibling)
+            if n == 0:
+                send(xb.at[t, c], xb.at[t, c], xs_sem.at[t, 4], xr_sem.at[t, c], row, z_pair * NC + core, inner)
+            send(xb.at[t, c], xb.at[t, c], xs_sem.at[t, 5 + n], xr_sem.at[t, c], row, sibling)
         for d in range(NZL):
             c = lax.rem(zl + d, NZL) * NC + (1 - core)
             arrived(xb.at[t, c], xs_sem.at[t, 0], xr_sem.at[t, c])
@@ -186,50 +215,34 @@
 
     def step1(t):
         send_l(t, 0, me_m, row_z)
-        send_r(t, 0, y, yrow(1))
-        send_r(t, 1, y, yrow(-1))
-        send_l(t, 1, me_m, xrow(1))
-        send_l(t, 2, me_m, xrow(-1))
+        send_r(t, 0, y, yrow(2))
+        send_r(t, 1, y, yrow(-2))
+        send_r(t, 2, y, yrow(1))
+        send_r(t, 3, y, yrow(-1))
+        send_l(t, 1, me_m, xrow(2))
+        send_l(t, 2, me_m, xrow(1))
+        send_l(t, 3, me_m, xrow(-1))
 
     def step2(t):
-        got_r(t, rslot(-1))
-        send_r(t, 2, rslot(-1), yrow(1))
-        got_r(t, rslot(1))
-        send_r(t, 3, rslot(1), yrow(-1))
-        got_l(t, lslot(False, -1))
-        got_l(t, lslot(False, 1))
+        got_r(t, rslot(-2))
         if t % 2 == 0:
-            send_l(t, 3, lslot(False, -1), xrow(1))
-        else:
-            send_l(t, 3, lslot(False, 1), xrow(-1))
-        got_l(t, lslot(True, 0))
-        send_l(t, 4, lslot(True, 0), xrow(1))
-        send_l(t, 5, lslot(True, 0), xrow(-1))
-
-    def step3(t):
-        got_r(t, rslot(-2))
+            send_r(t, 6, rslot(-2), yrow(2))
         send_r(t, 4, rslot(-2), yrow(1))
         got_r(t, rslot(2))
+        if t % 2 == 1:
+            send_r(t, 6, rslot(2), yrow(-2))
         send_r(t, 5, rslot(2), yrow(-1))
-        got_l(t, lslot(True, -1))
-        got_l(t, lslot(True, 1))
-        if t % 2 == 0:
-            send_l(t, 6, lslot(True, 1), xrow(-1))
-        else:
-            send_l(t, 6, lslot(True, -1), xrow(1))
-
-    def step4(t):
-        got_r(t, rslot(-3))
-        got_r(t, rslot(3))
-        if t % 2 == 0:
-            send_r(t, 6, rslot(-3), yrow(1))
-        else:
-            send_r(t, 6, rslot(3), yrow(-1))
-
-    def step5(t):
-        got_l(t, lslot(False, 2))
-        got_l(t, lslot(True, 2))
-        got_r(t, rslot(4))
+        got_l(t, lslot(True, 0))
+        send_l(t, 4, lslot(True, 0), xrow(2))
+        send_l(t, 5, lslot(True, 0), xrow(1))
+        send_l(t, 6, lslot(True, 0), xrow(-1))
+
+    def step3(t):
+        for d in (-1, 1, 2):
+            got_l(t, lslot(False, d))
+            got_l(t, lslot(True, d))
+        for d in (-1, 1, -3, 3, 4):
+            got_r(t, rslot(d))
         for h in range(8):
             a = lb[t, :, 16 * h:16 * h + 16, :].reshape(128, KC)
             b = rb[t, :, 16 * h:16 * h + 16, :].reshape(128, KC)
@@ -239,12 +252,14 @@
             else:
                 acc[h] += part
 
-    for wave in range(T + 4):
+    for wave in range(T + 2):
         if wave < T:
             gather_in(wave)
+            if wave + AHEAD < T:
+                send_in(wave + AHEAD)
             project(wave)
             step1(wave)
-        for back, step in ((4, step5), (3, step4), (2, step3), (1, step2)):
+        for back, step in ((1, step2), (2, step3)):
             if 0 <= wave - back < T:
                 step(wave - back)
 
@@ -260,6 +275,7 @@
         c = lax.rem(chan + s, NCH)
         send(es.at[c], er.at[chan], es_sem.at[s], er_sem.at[chan], row, c)
     er[chan] = es[chan]
+    drain(NCH - 1)
     for s in range(1, NCH):
         c = lax.rem(chan + s, NCH)
         arrived(er.at[c], es_sem.at[s], er_sem.at[c])
@@ -312,6 +328,8 @@
     def _():
         fr[me_m] = fs[chan]
 
+    drain(NCH - 1)
+
     for s in range(1, NCH):
         m = lax.rem(me_m + s, NCH)
         arrived(fr.at[m], fs_sem.at[s], fr_sem.at[m])
@@ -332,8 +350,7 @@
     for n in range(4):
         out[:, :, 128 * n:128 * n + 128] = o_f[n].reshape(16, 8, 128).astype(BF16)
 
-    for copy in sends:
-        copy.wait_send()
+    drain(0)
 
     @pl.when(jnp.logical_not(self_f))
     def _():
@@ -347,9 +364,19 @@
     return pl.pallas_call(
         kernel,
         out_shape=jax.ShapeDtypeStruct((16, 8, 512), BF16),
-        in_specs=[vm, sm] + [vm] * 8,
+        in_specs=[sm] + [pl.BlockSpec(memory_space=pltpu.HBM)] * 9,
         out_specs=vm,
         scratch_shapes=[
+            pltpu.VMEM((16, 8, 512), BF16),
+            pltpu.VMEM((1, 512), jnp.int32),
+            pltpu.VMEM((1, 16), BF16),
+            pltpu.VMEM((1, 16), BF16),
+            pltpu.VMEM((4, 16, 128), BF16),
+            pltpu.VMEM((1, 16), F32),
+            pltpu.VMEM((1, 16), F32),
+            pltpu.VMEM((128, 128), BF16),
+            pltpu.VMEM((16, 128), BF16),
+            dma((9,)),
             pltpu.VMEM((T, 128, KC), F32),
             pltpu.VMEM((T, NCH, 8, 16, KC), BF16),
             pltpu.VMEM((NCH, 16, 128), F32),
@@ -367,7 +394,7 @@
             pltpu.VMEM((512, 512), BF16),
             pltpu.VMEM((256, 64), BF16),
             pltpu.VMEM((4, 128, 128), F32),
-            dma((T, 7)), dma((T, NCH)),
+            dma((T, 8)), dma((T, NCH)),
             dma((NCH,)), dma((NCH,)),
             dma((T, 7)), dma((T, 8)),
             dma((T, 7)), dma((T, 8)),
@@ -375,11 +402,11 @@
             dma((NCH,)), dma((NCH,)),
         ],
         compiler_params=pltpu.CompilerParams(
-            collective_id=0, has_side_effects=True, vmem_limit_bytes=48 * 1024 * 1024
+            collective_id=0, has_side_effects=True, vmem_limit_bytes=60 * 1024 * 1024
         ),
     )(
+        token_mask,
         pair_in,
-        token_mask,
         token_mask.reshape(1, 512),
         in_gain.reshape(1, 16),
         in_bias.reshape(1, 16),

time: 70.4 us -> 59.8 us (0.85)
  Pallas kernels: 66.4 us -> 58.1 us
  local copies, waits for them, and re-layouts: 3.74 us -> 1.57 us
    pallas_call x1, Pallas kernels: 66.4 us -> 58.1 us  [body(): pl.pallas_call(kernel, out_shape=jax.ShapeDtypeStruct((16, 8, 512), BF16)...]
    unnamed x19 -> x1, local copies, waits for them, and re-layouts: 3.74 us -> 1.57 us
where the time goes in v2:
time: 59.8 us; the launch traced here: 59.7 us
  Pallas kernels  58.1 us (97%)
  local copies, waits for them, and re-layouts  1.57 us (3%)
    pallas_call x1, Pallas kernels, body(): pl.pallas_call(kernel, out_shape=jax.ShapeDtypeStruct((16, 8, 512), BF16)...  58.1 us
    unnamed x1, local copies, waits for them, and re-layouts  1.57 us

profile of v2, /device:TPU:1, one launch (start us, length us, event | category | flops | bytes accessed | tf_op | source)
XLA Modules:
  0.0 59.7 jit_solution(9461207811718596504)
XLA Ops:
  0.0 58.1 %shard_map.91 = bf16[16,8,512]{2,1,0:T(8,128)(2,1)} custom-call(s32[512]{0:T(512)} %tm_s.1, bf16[16,8,512]{2,1,0:T(8,128)(2,1)} %refs_0_.1, s32[1,512]{1,0:T(1,128)} %bitcast.8, bf16[1,16]{1,0:T(2,128)(2,1)} %bitcast.10, bf16[1,16]{1,0:T(2,128)(2,1)} %bitcast.11, bf16[4,16,128]{2,1,0:T(8,128)(2,1)} %bitcast.7, f32[1,16]{1,0:T(1,128)} %bitcast.12, ...), custom_call_target="tpu_custom_call" | custom-call | tf_op jit(solution)/shard_map/pallas_call | solution.py:364
  58.1 1.6 %copy.11 = bf16[16,8,512]{2,1,0:T(8,128)(2,1)} copy(bf16[16,8,512]{2,1,0:T(8,128)(2,1)} %shard_map.91) | data formatting | bytes 262144

commit v3 on v2

--- a/solution.py
+++ b/solution.py
@@ -12,6 +12,13 @@
 T = 4
 KC = 128
 AHEAD = 2
+ORDER = (
+    ("relay", 0), ("send", 2), ("relay", 1), ("in", 0), ("send", 3), ("proj", 0), ("s1", 0), ("relay", 2),
+    ("in", 1), ("proj", 1), ("s1", 1), ("relay", 3), ("s2", 0),
+    ("in", 2), ("proj", 2), ("s1", 2), ("s2l", 0), ("s2", 1),
+    ("in", 3), ("proj", 3), ("s1", 3), ("s2l", 1), ("s2", 2), ("s2l", 2), ("s2", 3), ("s3", 0), ("s3", 1),
+    ("s2l", 3), ("s3", 2), ("s3", 3),
+)
 F32 = jnp.float32
 BF16 = jnp.bfloat16
 
@@ -28,21 +35,21 @@
 
 
 def kernel(
-    tm_s, *refs,
+    *refs,
 ):
-    ins, (out, *vins), (sem_in, *rest) = refs[:9], refs[9:19], refs[19:]
-    run(tm_s, ins, out, vins, sem_in, *rest)
+    ins, (out, *vins), (sem_in, *rest) = refs[:10], refs[10:21], refs[21:]
+    run(ins, out, vins, sem_in, *rest)
 
 
 def run(
-    tm_s, ins, out, vins, sem_in,
+    ins, out, vins, sem_in,
     xf, xb, pm, gb, lr_f, lb, rb, acc, e_f, es, er, fs, fr, gate, perm, wot, o_f,
     xs_sem, xr_sem, ps_sem, pr_sem, ls_sem, lr_sem, rs_sem, rr_sem, es_sem, er_sem, fs_sem, fr_sem,
 ):
     loads = [pltpu.make_async_copy(a, b, sem_in.at[n]) for n, (a, b) in enumerate(zip(ins, vins))]
     for load in loads:
         load.start()
-    pair, tm_v, ig, ib, w, og, ob, wo, gw = vins
+    pair, ig, ib, og, ob, tm_v, w, wo, gw, tm_s = vins
     row = lax.axis_index("row")
     chan = lax.axis_index("chan")
     zh = lax.div(row, NY * NX)
@@ -109,7 +116,7 @@
             device_id=(row, sibling), device_id_type=MESH,
         ).wait_recv()
 
-    for load in loads:
+    for load in loads[:5]:
         load.wait()
 
     for t in range(T):
@@ -135,6 +142,9 @@
 
     for t in range(AHEAD):
         send_in(t)
+
+    for load in loads[5:]:
+        load.wait()
 
     ki = lax.broadcasted_iota(jnp.int32, (512, 512), 0)
     ni = lax.broadcasted_iota(jnp.int32, (512, 512), 1)
@@ -160,11 +170,20 @@
     gb[1] = jnp.broadcast_to(pmv[:, 1:2], (128, 128))
     row_valid = [tm_s[row * 8 + r].astype(F32) for r in range(8)]
 
+    early = []
+
+    def relay(t):
+        c = z_two * NC + core
+        arrived(xb.at[t, c], xs_sem.at[t, 0], xr_sem.at[t, c])
+        send(xb.at[t, c], xb.at[t, c], xs_sem.at[t, 4], xr_sem.at[t, c], row, z_pair * NC + core, inner)
+        early.append(t)
+
     def gather_in(t):
         for n, z in enumerate((z_two, z_pair, z_inner)):
             c = z * NC + core
-            arrived(xb.at[t, c], xs_sem.at[t, 0], xr_sem.at[t, c])
-            if n == 0:
+            if t not in early or n != 0:
+                arrived(xb.at[t, c], xs_sem.at[t, 0], xr_sem.at[t, c])
+            if n == 0 and t not in early:
                 send(xb.at[t, c], xb.at[t, c], xs_sem.at[t, 4], xr_sem.at[t, c], row, z_pair * NC + core, inner)
             send(xb.at[t, c], xb.at[t, c], xs_sem.at[t, 5 + n], xr_sem.at[t, c], row, sibling)
         for d in range(NZL):
@@ -232,6 +251,8 @@
         if t % 2 == 1:
             send_r(t, 6, rslot(2), yrow(-2))
         send_r(t, 5, rslot(2), yrow(-1))
+
+    def step2l(t):
         got_l(t, lslot(True, 0))
         send_l(t, 4, lslot(True, 0), xrow(2))
         send_l(t, 5, lslot(True, 0), xrow(1))
@@ -252,16 +273,8 @@
             else:
                 acc[h] += part
 
-    for wave in range(T + 2):
-        if wave < T:
-            gather_in(wave)
-            if wave + AHEAD < T:
-                send_in(wave + AHEAD)
-            project(wave)
-            step1(wave)
-        for back, step in ((1, step2), (2, step3)):
-            if 0 <= wave - back < T:
-                step(wave - back)
+    for step, t in ORDER:
+        {"in": gather_in, "send": send_in, "relay": relay, "proj": project, "s1": step1, "s2": step2, "s2l": step2l, "s3": step3}[step](t)
 
     lane = lax.broadcasted_iota(jnp.int32, (1, 128), 1)
     even = ((lane >> 3) & 1) == 0
@@ -359,24 +372,24 @@
 
 def body(pair_in, token_mask, in_gain, in_bias, in_weight, out_gain, out_bias, out_weight, gate_weight):
     vm = pl.BlockSpec(memory_space=pltpu.VMEM)
-    sm = pl.BlockSpec(memory_space=pltpu.SMEM)
     dma = pltpu.SemaphoreType.DMA
     return pl.pallas_call(
         kernel,
-        out_shape=jax.ShapeDtypeStruct((16, 8, 512), BF16),
-        in_specs=[sm] + [pl.BlockSpec(memory_space=pltpu.HBM)] * 9,
+        out_shape=pltpu.VMEM((16, 8, 512), BF16),
+        in_specs=[pl.BlockSpec(memory_space=pltpu.HBM)] * 10,
         out_specs=vm,
         scratch_shapes=[
             pltpu.VMEM((16, 8, 512), BF16),
-            pltpu.VMEM((1, 512), jnp.int32),
             pltpu.VMEM((1, 16), BF16),
             pltpu.VMEM((1, 16), BF16),
-            pltpu.VMEM((4, 16, 128), BF16),
             pltpu.VMEM((1, 16), F32),
             pltpu.VMEM((1, 16), F32),
+            pltpu.VMEM((1, 512), jnp.int32),
+            pltpu.VMEM((4, 16, 128), BF16),
             pltpu.VMEM((128, 128), BF16),
             pltpu.VMEM((16, 128), BF16),
-            dma((9,)),
+            pltpu.SMEM((512,), jnp.int32),
+            dma((10,)),
             pltpu.VMEM((T, 128, KC), F32),
             pltpu.VMEM((T, NCH, 8, 16, KC), BF16),
             pltpu.VMEM((NCH, 16, 128), F32),
@@ -405,16 +418,16 @@
             collective_id=0, has_side_effects=True, vmem_limit_bytes=60 * 1024 * 1024
         ),
     )(
-        token_mask,
         pair_in,
-        token_mask.reshape(1, 512),
         in_gain.reshape(1, 16),
         in_bias.reshape(1, 16),
-        jnp.transpose(in_weight, (0, 2, 1)),
         out_gain.reshape(1, 16),
         out_bias.reshape(1, 16),
+        token_mask.reshape(1, 512),
+        jnp.transpose(in_weight, (0, 2, 1)),
         out_weight,
         gate_weight.T,
+        token_mask,
     )
 
 

time: 59.8 us -> 55.5 us (0.928)
  Pallas kernels: 58.1 us -> 54.7 us
  local copies, waits for them, and re-layouts: 1.57 us -> 0.66 us
    pallas_call x1, Pallas kernels: 58.1 us -> 54.7 us  [body(): pl.pallas_call(kernel, out_shape=pltpu.VMEM((16, 8, 512), BF16), in_specs...]
    unnamed x1, local copies, waits for them, and re-layouts: 1.57 us -> 0.66 us
where the time goes in v3:
time: 55.5 us; the launch traced here: 55.4 us
  Pallas kernels  54.7 us (99%)
  local copies, waits for them, and re-layouts  0.66 us (1%)
    pallas_call x1, Pallas kernels, body(): pl.pallas_call(kernel, out_shape=pltpu.VMEM((16, 8, 512), BF16), in_specs...  54.7 us

profile of v3, /device:TPU:1, one launch (start us, length us, event | category | flops | bytes accessed | tf_op | source)
XLA Modules:
  0.0 55.4 jit_solution(14704518549804847922)
XLA Ops:
  0.0 54.7 %shard_map.91 = bf16[16,8,512]{2,1,0:T(8,128)(2,1)S(1)} custom-call(bf16[16,8,512]{2,1,0:T(8,128)(2,1)} %refs_0_.1, bf16[1,16]{1,0:T(2,128)(2,1)} %bitcast.10, bf16[1,16]{1,0:T(2,128)(2,1)} %bitcast.11, f32[1,16]{1,0:T(1,128)} %bitcast.12, f32[1,16]{1,0:T(1,128)} %bitcast.13, s32[1,512]{1,0:T(1,128)} %bitcast.8, bf16[4,16,128]{2,1,0:T(8,128)(2,1)} %bitcast.7, ...), custom_call_target="tpu_custom_call" | custom-call | tf_op jit(solution)/shard_map/pallas_call | solution.py:376
  54.8 0.7 %copy.11 = bf16[16,8,512]{2,1,0:T(8,128)(2,1)} copy(bf16[16,8,512]{2,1,0:T(8,128)(2,1)S(1)} %shard_map.91) | data formatting | bytes 262144

commit v4 on v3

--- a/solution.py
+++ b/solution.py
@@ -13,7 +13,7 @@
 KC = 128
 AHEAD = 2
 ORDER = (
-    ("relay", 0), ("send", 2), ("relay", 1), ("in", 0), ("send", 3), ("proj", 0), ("s1", 0), ("relay", 2),
+    ("relay", 0), ("send", 2), ("relay", 1), ("par", 0), ("in", 0), ("send", 3), ("proj", 0), ("s1", 0), ("relay", 2),
     ("in", 1), ("proj", 1), ("s1", 1), ("relay", 3), ("s2", 0),
     ("in", 2), ("proj", 2), ("s1", 2), ("s2l", 0), ("s2", 1),
     ("in", 3), ("proj", 3), ("s1", 3), ("s2l", 1), ("s2", 2), ("s2l", 2), ("s2", 3), ("s3", 0), ("s3", 1),
@@ -116,32 +116,36 @@
             device_id=(row, sibling), device_id_type=MESH,
         ).wait_recv()
 
-    for load in loads[:5]:
-        load.wait()
-
-    for t in range(T):
+    def prepare(t):
         xf[t] = pair[:, :, t * KC:(t + 1) * KC].astype(F32).reshape(128, KC)
         for r in range(8):
             xb[t, chan, r] = xf[t, pl.ds(r, 16, stride=8), :].astype(BF16)
+
+    def send_in(t):
+        for n, (z, when) in enumerate(((z_two, None), (z_inner, inner), (z_pair, None))):
+            send(xb.at[t, chan], xb.at[t, chan], xs_sem.at[t, 1 + n], xr_sem.at[t, chan], row, z * NC + core, when)
+        send(xb.at[t, chan], xb.at[t, chan], xs_sem.at[t, 0], xr_sem.at[t, chan], row, sibling)
+
+    for load in loads[1:5]:
+        load.wait()
     lane16 = lax.broadcasted_iota(jnp.int32, (16, 128), 1)
     cols = [column(v[...].astype(F32)) for v in (ig, ib, og, ob)]
     block = jnp.zeros((16, 128), F32)
     for n, col in enumerate(cols):
         block = jnp.where(lane16 == n, jnp.broadcast_to(col, (16, 128)), block)
     pm[chan] = block
-
+    loads[0].wait()
+    prepare(0)
     pl.semaphore_wait(bar, jnp.where(inner, NCH - 1 + 7, NCH - 1 + 7 + 2))
-
     for s in range(1, NCH):
         send(pm.at[chan], pm.at[chan], ps_sem.at[s], pr_sem.at[chan], row, lax.rem(chan + s, NCH))
-
-    def send_in(t):
-        for n, (z, when) in enumerate(((z_two, None), (z_inner, inner), (z_pair, None))):
-            send(xb.at[t, chan], xb.at[t, chan], xs_sem.at[t, 1 + n], xr_sem.at[t, chan], row, z * NC + core, when)
-        send(xb.at[t, chan], xb.at[t, chan], xs_sem.at[t, 0], xr_sem.at[t, chan], row, sibling)
-
-    for t in range(AHEAD):
+    send_in(0)
+    for t in range(1, AHEAD):
+        prepare(t)
         send_in(t)
+
+    for t in range(AHEAD, T):
+        prepare(t)
 
     for load in loads[5:]:
         load.wait()
@@ -162,12 +166,14 @@
         wot[par * 128:(par + 1) * 128, :] = dot(turned, pick).astype(BF16)
 
     wt = jnp.concatenate([w[...].reshape(64, 128), gw[...]], axis=0)
-    for s in range(1, NCH):
-        c = lax.rem(chan + s, NCH)
-        arrived(pm.at[c], ps_sem.at[s], pr_sem.at[c])
-    pmv = pm[...].reshape(128, 128)
-    gb[0] = jnp.broadcast_to(pmv[:, 0:1], (128, 128))
-    gb[1] = jnp.broadcast_to(pmv[:, 1:2], (128, 128))
+
+    def params(t):
+        for s in range(1, NCH):
+            c = lax.rem(chan + s, NCH)
+            arrived(pm.at[c], ps_sem.at[s], pr_sem.at[c])
+        for n in range(2):
+            gb[n] = jnp.broadcast_to(pm[...].reshape(128, 128)[:, n:n + 1], (128, 128))
+
     row_valid = [tm_s[row * 8 + r].astype(F32) for r in range(8)]
 
     early = []
@@ -210,7 +216,7 @@
         for r in range(8):
             lr_f[0, pl.ds(r, 16, stride=8), :] = left[:, r * KC:(r + 1) * KC]
             lr_f[1, pl.ds(r, 16, stride=8), :] = right[:, r * KC:(r + 1) * KC]
-            gate[r, :, t * KC:(t + 1) * KC] = g[:, r * KC:(r + 1) * KC]
+            gate[t, r] = g[:, r * KC:(r + 1) * KC]
         lb[t, me_m] = lr_f[0].astype(BF16)
         rb[t, y] = lr_f[1].astype(BF16)
 
@@ -274,7 +280,7 @@
                 acc[h] += part
 
     for step, t in ORDER:
-        {"in": gather_in, "send": send_in, "relay": relay, "proj": project, "s1": step1, "s2": step2, "s2l": step2l, "s3": step3}[step](t)
+        {"in": gather_in, "send": send_in, "relay": relay, "par": params, "proj": project, "s1": step1, "s2": step2, "s2l": step2l, "s3": step3}[step](t)
 
     lane = lax.broadcasted_iota(jnp.int32, (1, 128), 1)
     even = ((lane >> 3) & 1) == 0
@@ -302,7 +308,7 @@
     center = tri - mean[None, :, None, :]
     spread = across(jnp.sum(jnp.sum(center * center, axis=0), axis=1)) * (1.0 / 128)
     inverse = lax.rsqrt(spread + EPS)
-    e_f[0:128, :] = pmv
+    e_f[0:128, :] = pm[...].reshape(128, 128)
     g_e = e_f[pl.ds(0, 64, stride=2), :]
     g_o = e_f[pl.ds(1, 64, stride=2), :]
     gain = jnp.where(even, g_e[:, 2:3], g_o[:, 2:3])
@@ -343,23 +349,29 @@
 
     drain(NCH - 1)
 
-    for s in range(1, NCH):
-        m = lax.rem(me_m + s, NCH)
-        arrived(fr.at[m], fs_sem.at[s], fr_sem.at[m])
-
-    @pl.when(jnp.logical_not(self_f))
-    def _():
-        arrived(fr.at[me_m], fs_sem.at[0], fr_sem.at[me_m])
-
-    for z in range(NZH):
+    def finish(z):
         got = jnp.concatenate([fr[z * NX + i].reshape(64, 128) for i in range(NX)], axis=1)
         o = dot(got, perm[...])
         for q in range(4):
             for par in range(2):
                 r = 2 * q + par
-                val = o[16 * q:16 * q + 16, 256 * par:256 * par + 256] * gate[r, :, 256 * z:256 * z + 256]
                 for half in range(2):
-                    o_f[2 * z + half, pl.ds(r, 16, stride=8), :] = val[:, 128 * half:128 * half + 128]
+                    val = o[16 * q:16 * q + 16, 256 * par + 128 * half:256 * par + 128 * half + 128]
+                    o_f[2 * z + half, pl.ds(r, 16, stride=8), :] = val * gate[2 * z + half, r]
+
+    for s in range(1, NX):
+        m = zh * NX + lax.rem(x + s, NX)
+        arrived(fr.at[m], fs_sem.at[s], fr_sem.at[m])
+
+    @pl.when(jnp.logical_not(self_f))
+    def _():
+        arrived(fr.at[me_m], fs_sem.at[0], fr_sem.at[me_m])
+
+    finish(zh)
+    for i in range(NX):
+        m = (1 - zh) * NX + i
+        arrived(fr.at[m], fs_sem.at[NX + i], fr_sem.at[m])
+    finish(1 - zh)
     for n in range(4):
         out[:, :, 128 * n:128 * n + 128] = o_f[n].reshape(16, 8, 128).astype(BF16)
 
@@ -403,7 +415,7 @@
             pltpu.VMEM((8, 64, 128), BF16),
             pltpu.VMEM((8, 4, 16, 128), BF16),
             pltpu.VMEM((8, 4, 16, 128), BF16),
-            pltpu.VMEM((8, 16, 512), F32),
+            pltpu.VMEM((T, 8, 16, KC), F32),
             pltpu.VMEM((512, 512), BF16),
             pltpu.VMEM((256, 64), BF16),
             pltpu.VMEM((4, 128, 128), F32),

time: 55.5 us -> 55.4 us (level)
  no operation moved by 1% of the time
where the time goes in v4:
time: 55.4 us; the launch traced here: 55.3 us
  Pallas kernels  54.6 us (99%)
  local copies, waits for them, and re-layouts  0.66 us (1%)
    pallas_call x1, Pallas kernels, body(): pl.pallas_call(kernel, out_shape=pltpu.VMEM((16, 8, 512), BF16), in_specs...  54.6 us

profile of v4, /device:TPU:1, one launch (start us, length us, event | category | flops | bytes accessed | tf_op | source)
XLA Modules:
  0.0 55.3 jit_solution(6214790778041267553)
XLA Ops:
  0.0 54.6 %shard_map.91 = bf16[16,8,512]{2,1,0:T(8,128)(2,1)S(1)} custom-call(bf16[16,8,512]{2,1,0:T(8,128)(2,1)} %refs_0_.1, bf16[1,16]{1,0:T(2,128)(2,1)} %bitcast.10, bf16[1,16]{1,0:T(2,128)(2,1)} %bitcast.11, f32[1,16]{1,0:T(1,128)} %bitcast.12, f32[1,16]{1,0:T(1,128)} %bitcast.13, s32[1,512]{1,0:T(1,128)} %bitcast.8, bf16[4,16,128]{2,1,0:T(8,128)(2,1)} %bitcast.7, ...), custom_call_target="tpu_custom_call" | custom-call | tf_op jit(solution)/shard_map/pallas_call | solution.py:388
  54.6 0.7 %copy.11 = bf16[16,8,512]{2,1,0:T(8,128)(2,1)} copy(bf16[16,8,512]{2,1,0:T(8,128)(2,1)S(1)} %shard_map.91) | data formatting | bytes 262144

commit v5 on v4

--- a/solution.py
+++ b/solution.py
@@ -16,8 +16,8 @@
     ("relay", 0), ("send", 2), ("relay", 1), ("par", 0), ("in", 0), ("send", 3), ("proj", 0), ("s1", 0), ("relay", 2),
     ("in", 1), ("proj", 1), ("s1", 1), ("relay", 3), ("s2", 0),
     ("in", 2), ("proj", 2), ("s1", 2), ("s2l", 0), ("s2", 1),
-    ("in", 3), ("proj", 3), ("s1", 3), ("s2l", 1), ("s2", 2), ("s2l", 2), ("s2", 3), ("s3", 0), ("s3", 1),
-    ("s2l", 3), ("s3", 2), ("s3", 3),
+    ("in", 3), ("proj", 3), ("s1", 3), ("s2l", 1), ("s2", 2), ("s2l", 2), ("s2", 3), ("s3", 0), ("s2l", 3),
+    ("s3", 1), ("s3", 2), ("s3", 3),
 )
 F32 = jnp.float32
 BF16 = jnp.bfloat16

time: 55.4 us -> 55.2 us (level)
  no operation moved by 1% of the time
where the time goes in v5:
time: 55.2 us; the launch traced here: 55.1 us
  Pallas kernels  54.4 us (99%)
  local copies, waits for them, and re-layouts  0.66 us (1%)
    pallas_call x1, Pallas kernels, body(): pl.pallas_call(kernel, out_shape=pltpu.VMEM((16, 8, 512), BF16), in_specs...  54.4 us

profile of v5, /device:TPU:1, one launch (start us, length us, event | category | flops | bytes accessed | tf_op | source)
XLA Modules:
  0.0 55.1 jit_solution(3060658344762266006)
XLA Ops:
  0.0 54.4 %shard_map.91 = bf16[16,8,512]{2,1,0:T(8,128)(2,1)S(1)} custom-call(bf16[16,8,512]{2,1,0:T(8,128)(2,1)} %refs_0_.1, bf16[1,16]{1,0:T(2,128)(2,1)} %bitcast.10, bf16[1,16]{1,0:T(2,128)(2,1)} %bitcast.11, f32[1,16]{1,0:T(1,128)} %bitcast.12, f32[1,16]{1,0:T(1,128)} %bitcast.13, s32[1,512]{1,0:T(1,128)} %bitcast.8, bf16[4,16,128]{2,1,0:T(8,128)(2,1)} %bitcast.7, ...), custom_call_target="tpu_custom_call" | custom-call | tf_op jit(solution)/shard_map/pallas_call | solution.py:388
  54.4 0.7 %copy.11 = bf16[16,8,512]{2,1,0:T(8,128)(2,1)} copy(bf16[16,8,512]{2,1,0:T(8,128)(2,1)S(1)} %shard_map.91) | data formatting | bytes 262144
